TPU v7x, 256 devices: a whole 4x4x8 slice. The times are simulated.
256 devices in a mesh: row: 8 (over x, core), col: 32 (over y, z).
Axes of the slice: x: 4, y: 4, z: 8, core: 2. Of those that a mesh axis runs over, the one named last changes fastest.
Arguments:
- rhs: float32 [2048, 16, 8, 512], P('col', None, 'row'), may hold values from -6 to 6
- factor_rows: bfloat16 [2, 512, 16, 8, 512], P(None, 'col', None, 'row'), may hold values from -0.25 to 0.25
- diag_inverse: float32 [2, 512, 512], replicated, may hold values from -1.5 to 1.5, as said below
Outputs:
- solved: float32 [2, 2048, 512], P(None, 'col')
- updated: float32 [2048, 16, 8, 512], P('col', None, 'row')
Inputs may be any that keep to these rules, and one draw needn't show every extreme that they name: Each diag_inverse[s] is lower triangular with its diagonal between 0.5 and 1.5.
All inputs are finite; a program needn't handle non-finite values.
Results may differ from a plain program's by a relative error of at most 0.0031.
Values may be sent and summed in bfloat16 or wider, within the bound.
A program may use at most 128 MiB of HBM per device.

v0:
```python
import jax
import jax.numpy as jnp
from jax import lax
from jax.sharding import PartitionSpec as P


def spread(x, axis, root):
    mine = lax.axis_index(axis) == root
    return lax.psum(jnp.where(mine, x, jnp.zeros_like(x)), axis)


def on_device(rhs, factor_rows, diag_inverse):
    rows_here = rhs.shape[0]
    blocks_here = rhs.shape[1]
    block_width = rhs.shape[3]
    n_row = lax.axis_size("row")
    row_index = lax.axis_index("row")
    pending = rhs.reshape(rows_here, blocks_here * block_width)
    block_ids = jnp.arange(blocks_here * block_width) // block_width * n_row + row_index
    gathered = lax.all_gather(factor_rows, "col", axis=1, tiled=True)
    gathered = gathered.reshape(2, gathered.shape[1], blocks_here * block_width)
    top_block = blocks_here * n_row - 1
    results = []
    for step_index in range(2):
        current = top_block - step_index
        root_row = current % n_row
        candidate = jnp.dot(
            pending[:, -block_width:],
            diag_inverse[step_index],
            precision=lax.Precision.HIGHEST,
            preferred_element_type=jnp.float32,
        )
        solution = spread(candidate, "row", root_row)
        narrow = solution.astype(jnp.bfloat16)
        change = jnp.dot(narrow, gathered[step_index], preferred_element_type=jnp.float32)
        pending = pending - jnp.where(block_ids[None, :] < current, change, 0.0)
        results.append(solution)
    return (jnp.stack(results), pending.reshape(rhs.shape))


def solution(mesh):
    return jax.shard_map(
        on_device,
        mesh=mesh,
        in_specs=(P("col", None, "row", None), P(None, "col", None, "row", None), P()),
        out_specs=(P(None, "col", None), P("col", None, "row", None)),
        check_vma=False,
    )
```

profile of v0, /device:TPU:4, one launch (start us, length us, event | category | flops | bytes accessed | tf_op | source)
XLA Modules:
  0.0 268.1 jit_solution(7207519619204887052)
XLA Ops:
  8.0 0.0 all-gather.2.cloned.1.call-start
  8.0 0.7 all-gather.2.cloned.1.call-update
  8.7 0.0 all-reduce.3.cloned.1.call-start
  8.8 8.1 %reduce = f32[64,16,512]{2,1,0:T(8,128)} reduce(f32[64,16,1,512]{3,2,1,0:T(1,128)} %param.3, f32[]{:T(128)} %constant.41), dimensions={2}, to_apply=%param.3.reduce_sub_computation | reduce | bytes 4194308 | tf_op args[0]
  16.9 2.8 %copy.6 = f32[8,8,16,512]{3,1,2,0:T(8,128)S(1)} copy(f32[8,8,16,512]{3,2,1,0:T(8,128)} %bitcast.26) | data formatting | bytes 4194304
  19.7 2.6 convolution_select_fusion.3
  22.4 0.0 all-reduce.3.cloned.1.call-update
  22.4 0.0 all-reduce.5.cloned.1.call-start
  22.5 132.8 %all-gather.2.cloned.1.call-done = bf16[2,512,16,1,512]{4,2,3,1,0:T(8,128)(2,1)} async-done(((bf16[2,16,16,1,512]{4,2,3,1,0:T(8,128)(2,1)}), bf16[2,512,16,1,512]{4,2,3,1,0:T(8,128)(2,1)}) %all-gather.2.cloned.1.call-update) | async-done | bytes 16777232 | tf_op jit(solution)/shard_map/all_gather | solution.py:20
  155.3 11.6 %fusion.17 = (bf16[1,512,16,1,512]{4,2,3,1,0:T(8,128)(2,1)}, bf16[1,512,16,1,512]{4,2,3,1,0:T(8,128)(2,1)}) fusion(bf16[2,512,16,1,512]{4,2,3,1,0:T(8,128)(2,1)} %all-gather.2.cloned.1.call-done), kind=kLoop, calls=%fused_computation.26 | loop fusion | bytes 33554432 | tf_op jit(solution)/shard_map/slice | solution.py:35
  166.9 16.4 %copy.7 = bf16[64,8,16,512]{3,1,2,0:T(8,128)(2,1)} copy(bf16[64,8,16,512]{3,2,1,0:T(8,128)(2,1)} %bitcast.23) | data formatting | bytes 16777216
  183.3 5.2 %fusion = f32[64,8192]{1,0:T(8,128)S(1)} fusion(f32[64,8192]{1,0:T(8,128)S(1)} %bitcast.25, bf16[512,8192]{1,0:T(8,128)(2,1)} %bitcast.20, pred[8192]{0:T(1024)(128)(4,1)S(1)} %fusion.15, f32[64,512]{1,0:T(8,128)} %all-reduce.3.cloned.1.call-done), kind=kOutput, calls=%fused_computation.2 | convolution fusion | flops 537952256 | bytes 12722176 | tf_op jit(solution)/shard_map/dot_general | solution.py:35
  188.5 0.0 copy-start
  188.5 1.3 copy-done
  189.8 0.0 copy-done.2
  189.8 1.6 convolution_select_fusion.2
  191.4 0.0 all-reduce.5.cloned.1.call-update
  191.5 0.0 copy-start.1
  191.5 16.5 %copy.8 = bf16[64,8,16,512]{3,1,2,0:T(8,128)(2,1)} copy(bf16[64,8,16,512]{3,2,1,0:T(8,128)(2,1)} %bitcast.22) | data formatting | bytes 16777216
  208.0 40.8 %all-reduce.5.cloned.1.call-done = f32[64,512]{1,0:T(8,128)} async-done(((f32[64,512]{1,0:T(8,128)}), f32[64,512]{1,0:T(8,128)}) %all-reduce.5.cloned.1.call-update) | async-done | bytes 131088 | tf_op jit(solution)/shard_map/psum | solution.py:9
  248.8 6.4 %fusion.1 = f32[64,8192]{1,0:T(8,128)} fusion(f32[64,8192]{1,0:T(8,128)S(1)} %copy-done.1, bf16[512,8192]{1,0:T(8,128)(2,1)} %bitcast.21, pred[8192]{0:T(1024)(128)(4,1)S(1)} %fusion.14, f32[64,512]{1,0:T(8,128)} %all-reduce.5.cloned.1.call-done), kind=kOutput, calls=%fused_computation.3 | convolution fusion | flops 537952256 | bytes 12722176 | tf_op jit(solution)/shard_map/dot_general | solution.py:35
  255.2 4.7 %reshape.38 = f32[64,16,1,512]{3,2,1,0:T(1,128)} reshape(f32[64,8192]{1,0:T(8,128)} %fusion.1) | data formatting | bytes 4194304 | tf_op jit(solution)/shard_map/reshape | solution.py:38
  260.0 0.0 copy-done.4
  260.0 0.7 pad_maximum_fusion
  (8 shorter events, 0.0 us)
Async XLA Ops:
  8.0 147.3 %all-gather.2.cloned.1.call-start = ((), (), s32[]{:S(2)}) async-start(), calls=%async_computation.1 | async-start | bytes 17301504 | tf_op jit(solution)/shard_map/all_gather | solution.py:20
  8.7 174.6 %all-reduce.3.cloned.1.call-start = ((), (), s32[]{:S(2)}) async-start(), calls=%async_computation | async-start | bytes 262144 | tf_op jit(solution)/shard_map/psum | solution.py:9
  22.4 226.4 %all-reduce.5.cloned.1.call-start = ((), (), s32[]{:S(2)}) async-start(), calls=%async_computation.2 | async-start | bytes 262144 | tf_op jit(solution)/shard_map/psum | solution.py:9
  183.3 6.5 %copy-start.2 = (f32[2,512,512]{2,1,0:T(8,128)S(1)}, f32[2,512,512]{2,1,0:T(8,128)}, u32[]{:S(2)}) copy-start(f32[2,512,512]{2,1,0:T(8,128)} %param.5) | copy-start | bytes 6291460
  188.5 1.3 copy-start
  191.5 57.4 %copy-start.1 = (f32[64,8192]{1,0:T(8,128)S(1)}, f32[64,8192]{1,0:T(8,128)}, u32[]{:S(2)}) copy-start(f32[64,8192]{1,0:T(8,128)} %copy-done) | copy-start | bytes 6291460
  255.2 4.8 %copy-start.3 = (f32[64,512]{1,0:T(8,128)S(1)}, f32[64,512]{1,0:T(8,128)}, u32[]{:S(2)}) copy-start(f32[64,512]{1,0:T(8,128)} %all-reduce.3.cloned.1.call-done) | copy-start | bytes 393220
  255.2 4.8 %copy-start.4 = (f32[64,512]{1,0:T(8,128)S(1)}, f32[64,512]{1,0:T(8,128)}, u32[]{:S(2)}) copy-start(f32[64,512]{1,0:T(8,128)} %all-reduce.5.cloned.1.call-done) | copy-start | bytes 393220
Sparse Core Ops, SparseCore 0:
  11.8 143.5 all-gather.1
Sparse Core Ops, SparseCore 1:
  22.5 65.3 all-reduce.2
  191.5 57.2 all-reduce.4
where the time goes:
time: 272 us; the launch traced here: 268 us
  waiting for transfers between devices  174 us (64%)
  local copies, waits for them, and re-layouts  53.4 us (20%)
  matrix products  15.8 us (6%)
  between operations  15.5 us (6%)
  other arithmetic  8.88 us (3%)
    all_gather x1, waiting for transfers between devices, on_device(): gathered = lax.all_gather(factor_rows, 'col', axis=1, tiled=True)  133 us
    psum x2, waiting for transfers between devices, spread(): return lax.psum(jnp.where(mine, x, jnp.zeros_like(x)), axis)  40.8 us
    unnamed x13, local copies, waits for them, and re-layouts  37.1 us
    slice x1, local copies, waits for them, and re-layouts, on_device(): gathered[step_index]  11.6 us
    dot_general x2, matrix products, on_device(): jnp.dot(narrow, gathered[step_index], preferred_element_type=jnp.float32)  11.6 us
    unnamed x1, other arithmetic  8.13 us
  transfers between devices with their start and end apart: 3, of which 2 were waited for; matrix products, arithmetic and copies ran while one was open for 22% of the time, Pallas kernels for 0%

commit v1 on v0

v1 whole, which is shorter than its diff:
```python
import functools

import jax
import jax.numpy as jnp
from jax import lax
from jax.experimental import pallas as pl
from jax.experimental.pallas import tpu as pltpu
from jax.sharding import PartitionSpec as P

NY, NZ, NROW = 4, 8, 8
CHUNKS = 4
BF16, F32 = jnp.bfloat16, jnp.float32


def ring_order():
    hop_us, latency = 1.35, 1.5
    units = [(c, s) for c in range(CHUNKS) for s in range(2)]
    ready = {(u, 1): 2.0 * u[0] for u in units}
    events, now = [], 0.0
    pending = {(u, h) for u in units for h in range(1, 5)}
    arrived = {}
    while pending:
        can = [k for k in pending if k in ready and ready[k] <= now + 1e-9]
        if not can:
            now = min(ready[k] for k in pending if k in ready)
            continue
        pick = min(can, key=lambda k: (units.index(k[0]), k[1]))
        pending.remove(pick)
        events.append((now, "hop", pick[0], pick[1]))
        now += hop_us * (0.5 if pick[1] == 4 else 1.0)
        unit, hop = pick
        if hop < 4:
            ready[(unit, hop + 1)] = now + latency
        else:
            arrived[unit] = now + latency
    start = arrived[(0, 0)]
    events.append((start, "edge", None, None))
    events.append((start + 4.5, "solve1", None, None))
    events.append((start + 8.5, "narrow1", None, None))
    last = start + 11.5
    for c in range(CHUNKS):
        last = max(last, arrived[(c, 0)], arrived[(c, 1)])
        events.append((last, "chunk", c, None))
        last += 0.8
    events.sort(key=lambda e: e[0])
    return events


def kernel(
    x_hbm, f_hbm, d_hbm, sol_ref, upd_ref,
    x_v, f_v, f_wide, f_cut, d_v, buf, nar, low, edge_out, edge_in, back_out, back_in,
    in_sem, own_sem, ysend, yrecv, zsend, zrecv, rsend, rrecv, nsend, nrecv, esend, erecv, bsend, brecv,
):
    row = lax.axis_index("row")
    col = lax.axis_index("col")
    y = col // NZ
    z = col % NZ
    up, down = (z + 1) % NZ, (z + NZ - 1) % NZ

    def at(row_, y_, z_):
        return (row_, y_ * NZ + z_)

    def remote(src, dst, send, recv, device):
        return pltpu.make_async_remote_copy(
            src_ref=src, dst_ref=dst, send_sem=send, recv_sem=recv,
            device_id=device, device_id_type=pl.DeviceIdType.MESH,
        )

    f_in = pltpu.make_async_copy(f_hbm, f_v, in_sem.at[0])
    x_in = pltpu.make_async_copy(x_hbm, x_v, in_sem.at[1])
    d_in = pltpu.make_async_copy(d_hbm, d_v, in_sem.at[2])
    f_in.start()
    x_in.start()
    d_in.start()

    barrier = pltpu.get_barrier_semaphore()
    peers = [at(row, y, up), at(row, y, down)]
    peers += [at(row, (y + d) % NY, z) for d in range(1, NY)]
    peers += [at((row + d) % NROW, y, z) for d in range(1, NROW)]
    for peer in peers:
        pl.semaphore_signal(barrier, inc=1, device_id=peer, device_id_type=pl.DeviceIdType.MESH)

    f_in.wait()
    for l in range(4):
        f_wide[l] = f_v[:, l * 128:(l + 1) * 128].astype(F32)
    own = []
    for c in range(CHUNKS):
        for q in range(NY):
            j = 4 * q + 3 - c
            piece = jnp.concatenate([f_wide[l, pl.ds(j, 32, stride=16), :] for l in range(4)], axis=1)
            f_cut[q, c] = piece.astype(BF16).reshape(2, 16, 512)
        copy = pltpu.make_async_copy(f_cut.at[y, c], buf.at[c, :, y, z], own_sem.at[c])
        copy.start()
        own.append(copy)

    pl.semaphore_wait(barrier, len(peers))

    ycopies = {}
    for c in range(CHUNKS):
        for d in range(1, NY):
            to = (y + d) % NY
            copy = remote(
                f_cut.at[to, c], buf.at[c, :, y, z], ysend.at[c, d - 1], yrecv.at[c, d - 1], at(row, to, z)
            )
            copy.start()
            ycopies[c, d] = copy

    def block_of_rhs(j):
        return jnp.concatenate(
            [x_v[pl.ds(4 * j + l, 64, stride=64), :] for l in range(4)], axis=1
        )

    def spread_row(s, value, root):
        high = value.astype(BF16)
        nar[s, y] = high
        low[s] = (value - high.astype(F32)).astype(BF16)
        for part in range(2):
            for t in range(NROW):
                if t != root:
                    row_copy(s, part, t).start()

    def row_copy(s, part, t):
        ref = nar.at[s, y] if part == 0 else low.at[s]
        return remote(ref, ref, rsend.at[s, part, t], rrecv.at[s, part], at(t, y, z))

    def narrow_copy(s, d):
        ref = nar.at[s, y]
        return remote(ref, ref, nsend.at[s, d - 1], nrecv.at[s, d - 1], at(row, (y + d) % NY, z))

    def share_narrow(s, root):
        @pl.when(row != root)
        def _():
            row_copy(s, 0, 0).wait_recv()

        for d in range(1, NY):
            narrow_copy(s, d).start()

    def store_solved(s, root):
        @pl.when(row != root)
        def _():
            row_copy(s, 1, 0).wait_recv()

        sol_ref[s] = nar[s, y].astype(F32) + low[s].astype(F32)

    x_in.wait()
    d_in.wait()

    @pl.when(row == NROW - 1)
    def _():
        spread_row(
            0,
            jnp.dot(block_of_rhs(15), d_v[0], precision=lax.Precision.HIGHEST, preferred_element_type=F32),
            NROW - 1,
        )

    def hop_copy(unit, hop, way):
        c, s = unit
        n = c * 2 + s
        block = (z - (hop - 1) + NZ) % NZ if way == 0 else (z + hop - 1) % NZ
        if hop < 4:
            ref = buf.at[c, s, :, block]
        else:
            ref = buf.at[c, s, pl.ds(2 * way, 2), block]
        return remote(
            ref, ref, zsend.at[way, n, hop - 1], zrecv.at[way, n, hop - 1],
            at(row, y, up if way == 0 else down),
        )

    def matmul(c, s):
        return jnp.dot(
            nar[s].reshape(256, 512), buf[c, s].reshape(512, 512), preferred_element_type=F32
        )

    def edge_copy(d):
        to = (y + d) % NY
        return remote(edge_out.at[to], edge_in, esend.at[d - 1], erecv.at[0], at(row, to, z))

    def back_copy(c, d):
        to = (y + d) % NY
        return remote(
            back_out.at[c, to], back_in.at[c, y], bsend.at[c, d - 1], brecv.at[c, d - 1], at(row, to, z)
        )

    is_edge = jnp.logical_and(row == NROW - 2, y == NY - 1)
    waited = set()

    def wait_last(unit):
        for way in range(2):
            hop_copy(unit, 4, way).wait_recv()
        waited.add(unit)

    shared0 = False
    for _, kind, what, hop in ring_order():
        if kind == "hop":
            unit = what
            if hop == 1:
                if unit[1] == 0:
                    own[unit[0]].wait()
                    for d in range(1, NY):
                        ycopies[unit[0], d].wait_recv()
                for way in range(2):
                    hop_copy(unit, 1, way).start()
            else:
                if hop == 4 and not shared0:
                    share_narrow(0, NROW - 1)
                    shared0 = True
                for way in range(2):
                    hop_copy(unit, hop - 1, way).wait_recv()
                    hop_copy(unit, hop, way).start()
        elif kind == "edge":
            wait_last((0, 0))
            for d in range(1, NY):
                narrow_copy(0, d).wait_recv()

            @pl.when(is_edge)
            def _():
                edge_out[...] = matmul(0, 0).reshape(NY, 64, 512)
                for d in range(1, NY):
                    edge_copy(d).start()
                edge_in[...] = edge_out[NY - 1]

        elif kind == "solve1":

            @pl.when(row == NROW - 2)
            def _():
                @pl.when(y != NY - 1)
                def _():
                    edge_copy(1).wait_recv()

                spread_row(
                    1,
                    jnp.dot(
                        block_of_rhs(15) - edge_in[...], d_v[1],
                        precision=lax.Precision.HIGHEST, preferred_element_type=F32,
                    ),
                    NROW - 2,
                )

        elif kind == "narrow1":
            share_narrow(1, NROW - 2)
            store_solved(0, NROW - 1)
        else:
            c = what
            if c == 0:
                for d in range(1, NY):
                    narrow_copy(1, d).wait_recv()
            for s in range(2):
                if (c, s) not in waited:
                    wait_last((c, s))
            change = (matmul(c, 0) + matmul(c, 1)).astype(BF16).reshape(NY, 64, 512)
            back_out[c] = change
            for d in range(1, NY):
                back_copy(c, d).start()
            back_in[c, y] = back_out[c, y]

    store_solved(1, NROW - 2)
    for c in range(CHUNKS):
        for d in range(1, NY):
            back_copy(c, d).wait_recv()
        for q in range(NY):
            j = 4 * q + 3 - c

            def finish(change, j=j):
                for l in range(4):
                    rows = pl.ds(4 * j + l, 64, stride=64)
                    upd_ref[rows, :] = x_v[rows, :] - change[:, l * 128:(l + 1) * 128].astype(F32)

            if j < 15:
                finish(back_in[c, q])
            else:
                @pl.when(row < NROW - 2)
                def _():
                    finish(back_in[c, q])

                @pl.when(row == NROW - 2)
                def _():
                    finish(edge_in[...])

                @pl.when(row == NROW - 1)
                def _():
                    finish(jnp.zeros((64, 512), F32))

    for c in range(CHUNKS):
        for d in range(1, NY):
            ycopies[c, d].wait_send()
            back_copy(c, d).wait_send()
        for s in range(2):
            for hop in range(1, 5):
                for way in range(2):
                    hop_copy((c, s), hop, way).wait_send()
    for s in range(2):
        for d in range(1, NY):
            narrow_copy(s, d).wait_send()
    for s in range(2):
        root = NROW - 1 - s

        @pl.when(row == root)
        def _():
            for part in range(2):
                for t in range(NROW):
                    if t != root:
                        row_copy(s, part, t).wait_send()

    @pl.when(is_edge)
    def _():
        for d in range(1, NY):
            edge_copy(d).wait_send()


def on_device(rhs, factor_rows, diag_inverse):
    dma = pltpu.SemaphoreType.DMA
    any_space = pl.BlockSpec(memory_space=pl.ANY)
    solved, updated = pl.pallas_call(
        kernel,
        out_shape=(
            jax.ShapeDtypeStruct((2, 64, 512), F32),
            jax.ShapeDtypeStruct((4096, 128), F32),
        ),
        in_specs=[any_space] * 3,
        out_specs=[pl.BlockSpec(memory_space=pltpu.VMEM)] * 2,
        scratch_shapes=[
            pltpu.VMEM((4096, 128), F32),
            pltpu.VMEM((512, 512), BF16),
            pltpu.VMEM((4, 512, 128), F32),
            pltpu.VMEM((NY, CHUNKS, 2, 16, 512), BF16),
            pltpu.VMEM((2, 512, 512), F32),
            pltpu.VMEM((CHUNKS, 2, NY, NZ, 16, 512), BF16),
            pltpu.VMEM((2, NY, 64, 512), BF16),
            pltpu.VMEM((2, 64, 512), BF16),
            pltpu.VMEM((NY, 64, 512), F32),
            pltpu.VMEM((64, 512), F32),
            pltpu.VMEM((CHUNKS, NY, 64, 512), BF16),
            pltpu.VMEM((CHUNKS, NY, 64, 512), BF16),
            dma((3,)),
            dma((CHUNKS,)),
            dma((CHUNKS, NY - 1)),
            dma((CHUNKS, NY - 1)),
            dma((2, CHUNKS * 2, 4)),
            dma((2, CHUNKS * 2, 4)),
            dma((2, 2, NROW)),
            dma((2, 2)),
            dma((2, NY - 1)),
            dma((2, NY - 1)),
            dma((NY - 1,)),
            dma((1,)),
            dma((CHUNKS, NY - 1)),
            dma((CHUNKS, NY - 1)),
        ],
        compiler_params=pltpu.CompilerParams(
            collective_id=0, has_side_effects=True, vmem_limit_bytes=48 * 1024 * 1024
        ),
        name="back_substitution",
    )(
        rhs.reshape(4096, 128),
        factor_rows.reshape(512, 512),
        diag_inverse,
    )
    return solved, updated.reshape(rhs.shape)


def solution(mesh):
    return jax.shard_map(
        on_device,
        mesh=mesh,
        in_specs=(P("col", None, "row", None), P(None, "col", None, "row", None), P()),
        out_specs=(P(None, "col", None), P("col", None, "row", None)),
        check_vma=False,
    )
```

time: 272 us -> 77 us (0.28); the launches traced: 268 us -> 76.2 us
  waiting for transfers between devices: 174 us -> 0 us
  Pallas kernels: 0 us -> 70.9 us
  local copies, waits for them, and re-layouts: 53.4 us -> 4.65 us
  matrix products: 15.8 us -> 0 us
  between operations: 15.5 us -> 0.65 us
  other arithmetic: 8.88 us -> 0 us
    all_gather x1 -> x0, waiting for transfers between devices: 133 us -> none  [on_device(): gathered = lax.all_gather(factor_rows, 'col', axis=1, tiled=True)]
    pallas_call x0 -> x1, Pallas kernels: none -> 70.9 us  [on_device(): pl.pallas_call(kernel, out_shape=(jax.ShapeDtypeStruct((2, 64, 512), F32)...]
    psum x2 -> x0, waiting for transfers between devices: 40.8 us -> none  [spread(): return lax.psum(jnp.where(mine, x, jnp.zeros_like(x)), axis)]
    unnamed x13 -> x6, local copies, waits for them, and re-layouts: 37.1 us -> 4.65 us
    dot_general x4 -> x0, matrix products: 15.8 us -> none  [the longest x2 11.6 us: on_device(): jnp.dot(narrow, gathered[step_index], preferred_element_type=jnp.float32)]
    slice x1 -> x0, local copies, waits for them, and re-layouts: 11.6 us -> none  [on_device(): gathered[step_index]]
    unnamed x1 -> x0, other arithmetic: 8.13 us -> none
    reshape x1 -> x0, local copies, waits for them, and re-layouts: 4.75 us -> none  [on_device(): return (jnp.stack(results), pending.reshape(rhs.shape))]
  transfers between devices with their start and end apart: 3 -> 0, of which waited for: 2 -> 0; matrix products, arithmetic and copies ran while one was open for 22% -> 0% of each run, Pallas kernels for 0% -> 0%
where the time goes in v1:
time: 77 us; the launch traced here: 76.2 us
  Pallas kernels  70.9 us (92%)
  local copies, waits for them, and re-layouts  4.65 us (6%)
    pallas_call x1, Pallas kernels, on_device(): pl.pallas_call(kernel, out_shape=(jax.ShapeDtypeStruct((2, 64, 512), F32)...  70.9 us
    unnamed x6, local copies, waits for them, and re-layouts  4.65 us

profile of v1, /device:TPU:4, one launch (start us, length us, event | category | flops | bytes accessed | tf_op | source)
XLA Modules:
  0.0 76.2 jit_solution(1365909756925196232)
XLA Ops:
  0.6 0.0 copy-start
  0.6 1.6 %copy-done = f32[64,16,1,512]{3,2,1,0:T(1,128)S(1)} copy-done((f32[64,16,1,512]{3,2,1,0:T(1,128)S(1)}, f32[64,16,1,512]{3,2,1,0:T(1,128)}, u32[]{:S(2)}) %copy-start) | copy-done | bytes 2097176
  2.2 0.0 copy-start.1
  2.2 1.0 %copy-done.1 = bf16[2,16,16,1,512]{4,2,3,1,0:T(8,128)(2,1)S(1)} copy-done((bf16[2,16,16,1,512]{4,2,3,1,0:T(8,128)(2,1)S(1)}, bf16[2,16,16,1,512]{4,2,3,1,0:T(8,128)(2,1)}, u32[]{:S(2)}) %copy-start.1) | copy-done | bytes 524312
  3.3 70.9 %back_substitution.1 = (f32[2,64,512]{2,1,0:T(8,128)S(1)}, f32[4096,128]{1,0:T(8,128)S(1)}) custom-call(f32[4096,128]{1,0:T(8,128)S(1)} %bitcast.3, bf16[512,512]{1,0:T(8,128)(2,1)S(1)} %bitcast.5, f32[2,512,512]{2,1,0:T(8,128)} %d_hbm.1), custom_call_target="tpu_custom_call" | custom-call | tf_op jit(solution)/shard_map/back_substitution/pallas_call | solution.py:313
  74.2 0.7 copy.8
  74.9 1.3 %copy.9 = f32[64,16,1,512]{3,2,1,0:T(1,128)} copy(f32[64,16,1,512]{3,2,1,0:T(1,128)S(1)} %bitcast.4) | data formatting | bytes 4194304
Async XLA Ops:
  0.6 1.6 %copy-start = (f32[64,16,1,512]{3,2,1,0:T(1,128)S(1)}, f32[64,16,1,512]{3,2,1,0:T(1,128)}, u32[]{:S(2)}) copy-start(f32[64,16,1,512]{3,2,1,0:T(1,128)} %param.3) | copy-start | bytes 6291460
  2.2 1.0 %copy-start.1 = (bf16[2,16,16,1,512]{4,2,3,1,0:T(8,128)(2,1)S(1)}, bf16[2,16,16,1,512]{4,2,3,1,0:T(8,128)(2,1)}, u32[]{:S(2)}) copy-start(bf16[2,16,16,1,512]{4,2,3,1,0:T(8,128)(2,1)} %param.4) | copy-start | bytes 1572868

commit v2 on v1

v2 whole, which is shorter than its diff:
```python
import functools

import jax
import jax.numpy as jnp
from jax import lax
from jax.experimental import pallas as pl
from jax.experimental.pallas import tpu as pltpu
from jax.sharding import PartitionSpec as P

NY, NZ, NROW = 4, 8, 8
CHUNKS = 4
UNITS = "ABCDEFGH"
ROW_TARGETS = (2, 3, 0, 1, 4, 5, 6, 7)
BF16, F32 = jnp.bfloat16, jnp.float32
ORDER = (
    "A1", "B1", "C1", "A2", "E1", "D1", "A3", "B2", "F1", "A4", "G1",
    "C2", "B3", "H1", "edge", "C3", "D2", "B4", "F2", "E2", "C4", "solve",
    "D3", "F3", "G2", "share", "E3", "D4", "F4", "H2", "c0", "E4", "G3",
    "c1", "H3", "c2", "G4", "H4", "f0", "f1", "c3", "f2", "f3",
)


def kernel(
    x_hbm, f_hbm, d_hbm, sol_ref, upd_ref,
    x_v, f_v, f_wide, f_cut, d_v, d_cut, buf, nar, lhs, low, edge_out, edge_in, back_out, back_in,
    in_sem, own_sem, ysend, yrecv, osend, orecv, zsend, zrecv, rsend, rrecv, nsend, nrecv,
    esend, erecv, bsend, brecv,
):
    row = lax.axis_index("row")
    col = lax.axis_index("col")
    y = col // NZ
    z = col % NZ
    up, down = (z + 1) % NZ, (z + NZ - 1) % NZ
    first_root, second_root = NROW - 1, NROW - 2

    def at(row_, y_, z_):
        return (row_, y_ * NZ + z_)

    def remote(src, dst, send, recv, device):
        return pltpu.make_async_remote_copy(
            src_ref=src, dst_ref=dst, send_sem=send, recv_sem=recv,
            device_id=device, device_id_type=pl.DeviceIdType.MESH,
        )

    def signal(device):
        pl.semaphore_signal(barrier, inc=1, device_id=device, device_id_type=pl.DeviceIdType.MESH)

    barrier = pltpu.get_barrier_semaphore()
    signal(at(row, y, up))
    signal(at(row, y, down))
    for d in range(1, NY):
        signal(at(row, (y + d) % NY, z))
    for root in (first_root, second_root):
        for t in range(NROW):
            if t != root:
                if t < second_root:
                    @pl.when(row == root)
                    def _(t=t):
                        signal(at(t, y, z))

                    @pl.when(row == t)
                    def _(root=root):
                        signal(at(root, y, z))
                else:
                    @pl.when(row == root)
                    def _(t=t):
                        signal(at(t, y, z))

    f_in = pltpu.make_async_copy(f_hbm, f_v, in_sem.at[0])
    x_in = pltpu.make_async_copy(x_hbm, x_v, in_sem.at[1])
    d_in = pltpu.make_async_copy(d_hbm.at[jnp.where(row == first_root, 0, 1)], d_v, in_sem.at[2])
    f_in.start()
    d_in.start()
    x_in.start()

    f_in.wait()
    for l in range(4):
        f_wide[l] = f_v[:, l * 128:(l + 1) * 128].astype(F32)
    for c in range(CHUNKS):
        for q in range(NY):
            j = 4 * q + 3 - c
            piece = jnp.concatenate([f_wide[l, pl.ds(j, 32, stride=16), :] for l in range(4)], axis=1)
            f_cut[q, c] = piece.astype(BF16).reshape(2, 16, 512)
    own = pltpu.make_async_copy(f_cut.at[y], buf.at[:, :, 0, z], own_sem)
    own.start()

    @pl.when(row >= second_root)
    def _():
        pl.semaphore_wait(barrier, 2 + NY - 1 + NROW - 1)

    @pl.when(row < second_root)
    def _():
        pl.semaphore_wait(barrier, 2 + NY - 1 + 2)

    def y_copy(c, d):
        to = (y + d) % NY
        return remote(
            f_cut.at[to, c], buf.at[c, :, NY - d, z], ysend.at[c, d - 1], yrecv.at[c, d - 1], at(row, to, z)
        )

    def own_copy(part, way):
        chunks = pl.ds(0, 1) if part == 0 else pl.ds(1, CHUNKS - 1)
        return remote(
            f_cut.at[y, chunks], buf.at[chunks, :, 0, z], osend.at[part, way], orecv.at[part, way],
            at(row, y, up if way == 0 else down),
        )

    for c in range(CHUNKS):
        for d in range(1, NY):
            y_copy(c, d).start()
        if c < 2:
            for way in range(2):
                own_copy(c, way).start()

    def block_of_rhs(j):
        return jnp.concatenate(
            [x_v[pl.ds(4 * j + l, 64, stride=64), :] for l in range(4)], axis=1
        )

    def halves(value):
        high = value.astype(BF16)
        return high, (value - high.astype(F32)).astype(BF16)

    def times_inverse(value):
        high, rest = halves(value)
        dot = functools.partial(jnp.dot, preferred_element_type=F32)
        return dot(high, d_cut[0]) + (dot(high, d_cut[1]) + dot(rest, d_cut[0]))

    def spread_row(s, value, root):
        nar[s, y], low[s] = halves(value)
        for part in range(2):
            for t in ROW_TARGETS:
                if t != root:
                    row_copy(s, part, t).start()

    def row_copy(s, part, t):
        ref = nar.at[s, y] if part == 0 else low.at[s]
        return remote(ref, ref, rsend.at[s, part, t], rrecv.at[s, part], at(t, y, z))

    def narrow_copy(s, d):
        ref = nar.at[s, y]
        return remote(ref, ref, nsend.at[s, d - 1], nrecv.at[s, d - 1], at(row, (y + d) % NY, z))

    def share_narrow(s, root):
        @pl.when(row != root)
        def _():
            row_copy(s, 0, 0).wait_recv()

        for d in range(1, NY):
            narrow_copy(s, d).start()

    def take_narrow(s):
        for d in range(1, NY):
            narrow_copy(s, d).wait_recv()
        for d in range(NY):
            columns = pl.ds(pl.multiple_of((y + d) % NY * 128, 128), 128)
            for q in range(NY):
                lhs[q * 64:(q + 1) * 64, s * 512 + d * 128:s * 512 + (d + 1) * 128] = nar[s, q, :, columns]

    def store_solved(s, root):
        @pl.when(row != root)
        def _():
            row_copy(s, 1, 0).wait_recv()

        sol_ref[s] = nar[s, y].astype(F32) + low[s].astype(F32)

    d_in.wait()
    x_in.wait()

    @pl.when(row >= second_root)
    def _():
        for i in range(4):
            rows = slice(i * 128, (i + 1) * 128)
            d_cut[0, rows], d_cut[1, rows] = halves(d_v[rows])

    @pl.when(row == first_root)
    def _():
        spread_row(0, times_inverse(block_of_rhs(15)), first_root)

    def hop_copy(unit, hop, way):
        c, s = unit
        n = c * 2 + s
        block = (z - (hop - 1) + NZ) % NZ if way == 0 else (z + hop - 1) % NZ
        if hop == 1:
            ref = buf.at[c, s, pl.ds(1, NY - 1), block]
        elif hop < 4:
            ref = buf.at[c, s, :, block]
        else:
            ref = buf.at[c, s, pl.ds(2 * way, 2), block]
        return remote(
            ref, ref, zsend.at[way, n, hop - 1], zrecv.at[way, n, hop - 1],
            at(row, y, up if way == 0 else down),
        )

    def edge_copy(d):
        to = (y + d) % NY
        return remote(edge_out.at[to], edge_in, esend.at[d - 1], erecv.at[0], at(row, to, z))

    def back_copy(c, d):
        to = (y + d) % NY
        return remote(
            back_out.at[c, to], back_in.at[c, y], bsend.at[c, d - 1], brecv.at[c, d - 1], at(row, to, z)
        )

    is_edge = jnp.logical_and(row == second_root, y == NY - 1)

    def wait_last(unit):
        for way in range(2):
            hop_copy(unit, 4, way).wait_recv()

    def subtract(j, change):
        for l in range(4):
            rows = pl.ds(4 * j + l, 64, stride=64)
            upd_ref[rows, :] = x_v[rows, :] - change[:, l * 128:(l + 1) * 128].astype(F32)

    own_seen, y_seen = set(), set()
    own.wait()
    for step in ORDER:
        if step[0] in UNITS and len(step) == 2:
            n = UNITS.index(step[0])
            unit, hop = (n // 2, n % 2), int(step[1])
            c = unit[0]
            if hop == 1 and c not in y_seen:
                y_seen.add(c)
                for d in range(1, NY):
                    y_copy(c, d).wait_recv()
            if hop == 2 and min(c, 1) not in own_seen:
                own_seen.add(min(c, 1))
                for way in range(2):
                    own_copy(min(c, 1), way).wait_recv()
            if step == "A3":
                share_narrow(0, first_root)
            for way in range(2):
                if hop > 1:
                    hop_copy(unit, hop - 1, way).wait_recv()
                hop_copy(unit, hop, way).start()
        elif step == "edge":
            take_narrow(0)
            wait_last((0, 0))

            @pl.when(is_edge)
            def _():
                product = jnp.dot(
                    lhs[:, :512], buf[0, 0].reshape(512, 512), preferred_element_type=F32
                )
                edge_out[...] = product.reshape(NY, 64, 512)
                for d in range(1, NY):
                    edge_copy(d).start()
                edge_in[...] = edge_out[NY - 1]

            store_solved(0, first_root)

        elif step == "solve":

            @pl.when(row == second_root)
            def _():
                @pl.when(y != NY - 1)
                def _():
                    edge_copy(1).wait_recv()

                spread_row(1, times_inverse(block_of_rhs(15) - edge_in[...]), second_root)

        elif step == "share":
            share_narrow(1, second_root)
        elif step[0] == "c":
            c = int(step[1])
            if c == 0:
                take_narrow(1)
            for s in range(2):
                if (c, s) != (0, 0):
                    wait_last((c, s))
            change = jnp.dot(lhs[...], buf[c].reshape(1024, 512), preferred_element_type=F32)
            back_out[c] = change.astype(BF16).reshape(NY, 64, 512)
            for d in range(1, NY):
                back_copy(c, d).start()
            back_in[c, y] = back_out[c, y]
        else:
            c = int(step[1])
            if c == 0:
                store_solved(1, second_root)
            for d in range(1, NY):
                back_copy(c, d).wait_recv()
            for q in range(NY):
                j = 4 * q + 3 - c
                if j < 15:
                    subtract(j, back_in[c, q])
                else:
                    @pl.when(row < second_root)
                    def _():
                        subtract(15, back_in[0, NY - 1])

                    @pl.when(row == second_root)
                    def _():
                        subtract(15, edge_in[...])

                    @pl.when(row == first_root)
                    def _():
                        subtract(15, jnp.zeros((64, 512), F32))

    for c in range(CHUNKS):
        for d in range(1, NY):
            y_copy(c, d).wait_send()
            back_copy(c, d).wait_send()
        for s in range(2):
            for hop in range(1, 5):
                for way in range(2):
                    hop_copy((c, s), hop, way).wait_send()
    for part in range(2):
        for way in range(2):
            own_copy(part, way).wait_send()
    for s in range(2):
        for d in range(1, NY):
            narrow_copy(s, d).wait_send()
    for s in range(2):
        root = NROW - 1 - s

        @pl.when(row == root)
        def _():
            for part in range(2):
                for t in range(NROW):
                    if t != root:
                        row_copy(s, part, t).wait_send()

    @pl.when(is_edge)
    def _():
        for d in range(1, NY):
            edge_copy(d).wait_send()


def on_device(rhs, factor_rows, diag_inverse):
    dma = pltpu.SemaphoreType.DMA
    any_space = pl.BlockSpec(memory_space=pl.ANY)
    in_hbm = functools.partial(pltpu.with_memory_space_constraint, memory_space=pltpu.HBM)
    solved, updated = pl.pallas_call(
        kernel,
        out_shape=(
            pltpu.VMEM((2, 64, 512), F32),
            pltpu.VMEM((4096, 128), F32),
        ),
        in_specs=[any_space] * 3,
        out_specs=[pl.BlockSpec(memory_space=pltpu.VMEM)] * 2,
        scratch_shapes=[
            pltpu.VMEM((4096, 128), F32),
            pltpu.VMEM((512, 512), BF16),
            pltpu.VMEM((4, 512, 128), F32),
            pltpu.VMEM((NY, CHUNKS, 2, 16, 512), BF16),
            pltpu.VMEM((512, 512), F32),
            pltpu.VMEM((2, 512, 512), BF16),
            pltpu.VMEM((CHUNKS, 2, NY, NZ, 16, 512), BF16),
            pltpu.VMEM((2, NY, 64, 512), BF16),
            pltpu.VMEM((256, 1024), BF16),
            pltpu.VMEM((2, 64, 512), BF16),
            pltpu.VMEM((NY, 64, 512), F32),
            pltpu.VMEM((64, 512), F32),
            pltpu.VMEM((CHUNKS, NY, 64, 512), BF16),
            pltpu.VMEM((CHUNKS, NY, 64, 512), BF16),
            dma((3,)),
            dma,
            dma((CHUNKS, NY - 1)),
            dma((CHUNKS, NY - 1)),
            dma((2, 2)),
            dma((2, 2)),
            dma((2, CHUNKS * 2, 4)),
            dma((2, CHUNKS * 2, 4)),
            dma((2, 2, NROW)),
            dma((2, 2)),
            dma((2, NY - 1)),
            dma((2, NY - 1)),
            dma((NY - 1,)),
            dma((1,)),
            dma((CHUNKS, NY - 1)),
            dma((CHUNKS, NY - 1)),
        ],
        compiler_params=pltpu.CompilerParams(
            collective_id=0, has_side_effects=True, vmem_limit_bytes=48 * 1024 * 1024
        ),
        name="back_substitution",
    )(
        in_hbm(rhs.reshape(4096, 128)),
        in_hbm(factor_rows.reshape(512, 512)),
        in_hbm(diag_inverse),
    )
    return solved, updated.reshape(rhs.shape)


def solution(mesh):
    return jax.shard_map(
        on_device,
        mesh=mesh,
        in_specs=(P("col", None, "row", None), P(None, "col", None, "row", None), P()),
        out_specs=(P(None, "col", None), P("col", None, "row", None)),
        check_vma=False,
    )
```

time: 77 us -> 67.3 us (0.87)
  Pallas kernels: 70.9 us -> 64.5 us
  local copies, waits for them, and re-layouts: 4.65 us -> 2.02 us
    pallas_call x1, Pallas kernels: 70.9 us -> 64.5 us  [on_device(): pl.pallas_call(kernel, out_shape=(pltpu.VMEM((2, 64, 512), F32), pltpu.VM...]
    unnamed x6 -> x2, local copies, waits for them, and re-layouts: 4.65 us -> 2.02 us
where the time goes in v2:
time: 67.3 us; the launch traced here: 67.2 us
  Pallas kernels  64.5 us (96%)
  local copies, waits for them, and re-layouts  2.02 us (3%)
    pallas_call x1, Pallas kernels, on_device(): pl.pallas_call(kernel, out_shape=(pltpu.VMEM((2, 64, 512), F32), pltpu.VM...  64.5 us
    unnamed x2, local copies, waits for them, and re-layouts  2.02 us

profile of v2, /device:TPU:4, one launch (start us, length us, event | category | flops | bytes accessed | tf_op | source)
XLA Modules:
  0.0 67.2 jit_solution(4328096456580700910)
XLA Ops:
  0.6 64.5 %back_substitution.1 = (f32[2,64,512]{2,1,0:T(8,128)S(1)}, f32[4096,128]{1,0:T(8,128)S(1)}) custom-call(f32[4096,128]{1,0:T(8,128)} %bitcast.4, bf16[512,512]{1,0:T(8,128)(2,1)} %bitcast.5, f32[2,512,512]{2,1,0:T(8,128)} %d_hbm.1), custom_call_target="tpu_custom_call" | custom-call | tf_op jit(solution)/shard_map/back_substitution/pallas_call | solution.py:334
  65.2 0.7 %copy.8 = f32[2,64,512]{2,1,0:T(8,128)} copy(f32[2,64,512]{2,1,0:T(8,128)S(1)} %get-tuple-element.8) | data formatting | bytes 524288
  65.9 1.3 %copy.9 = f32[64,16,1,512]{3,2,1,0:T(1,128)} copy(f32[64,16,1,512]{3,2,1,0:T(1,128)S(1)} %bitcast.3) | data formatting | bytes 4194304

commit v3 on v2

--- a/solution.py
+++ b/solution.py
@@ -10,21 +10,24 @@
 NY, NZ, NROW = 4, 8, 8
 CHUNKS = 4
 UNITS = "ABCDEFGH"
-ROW_TARGETS = (2, 3, 0, 1, 4, 5, 6, 7)
+ROW_TARGETS = (6, 2, 3, 0, 1, 4, 5, 7)
+FAR = (2, 3, 4, 5, 6)
 BF16, F32 = jnp.bfloat16, jnp.float32
+BOUNDS = (0, 5, 10, 14, 16)
 ORDER = (
-    "A1", "B1", "C1", "A2", "E1", "D1", "A3", "B2", "F1", "A4", "G1",
-    "C2", "B3", "H1", "edge", "C3", "D2", "B4", "F2", "E2", "C4", "solve",
-    "D3", "F3", "G2", "share", "E3", "D4", "F4", "H2", "c0", "E4", "G3",
-    "c1", "H3", "c2", "G4", "H4", "f0", "f1", "c3", "f2", "f3",
+    "A1", "B1", "C1", "e0", "G1", "D1", "e1", "H1", "C2", "D2", "edge",
+    "G2", "B2", "E1", "A2", "D3", "F1", "B3", "C3", "solve", "D4", "A3",
+    "E2", "n0", "F2", "C4", "share", "A4", "B4", "F3", "E3", "H2", "c1",
+    "G3", "c0", "F4", "E4", "H3", "G4", "c2", "H4", "c3", "f0", "f1",
+    "f2", "f3",
 )
 
 
 def kernel(
     x_hbm, f_hbm, d_hbm, sol_ref, upd_ref,
-    x_v, f_v, f_wide, f_cut, d_v, d_cut, buf, nar, lhs, low, edge_out, edge_in, back_out, back_in,
+    x_v, f_v, f_wide, f_cut, d_v, d_cut, buf, edge_f, nar, lhs, low, edge_out, edge_in, back_out, back_in,
     in_sem, own_sem, ysend, yrecv, osend, orecv, zsend, zrecv, rsend, rrecv, nsend, nrecv,
-    esend, erecv, bsend, brecv,
+    esend, erecv, pysend, pyrecv, pzsend, pzrecv, bsend, brecv,
 ):
     row = lax.axis_index("row")
     col = lax.axis_index("col")
@@ -66,6 +69,11 @@
                     def _(t=t):
                         signal(at(t, y, z))
 
+    @pl.when(row == second_root)
+    def _():
+        for d in FAR:
+            signal(at(row, y, (z + d) % NZ))
+
     f_in = pltpu.make_async_copy(f_hbm, f_v, in_sem.at[0])
     x_in = pltpu.make_async_copy(x_hbm, x_v, in_sem.at[1])
     d_in = pltpu.make_async_copy(d_hbm.at[jnp.where(row == first_root, 0, 1)], d_v, in_sem.at[2])
@@ -76,41 +84,39 @@
     f_in.wait()
     for l in range(4):
         f_wide[l] = f_v[:, l * 128:(l + 1) * 128].astype(F32)
-    for c in range(CHUNKS):
-        for q in range(NY):
-            j = 4 * q + 3 - c
-            piece = jnp.concatenate([f_wide[l, pl.ds(j, 32, stride=16), :] for l in range(4)], axis=1)
-            f_cut[q, c] = piece.astype(BF16).reshape(2, 16, 512)
+    for q in range(NY):
+        for j in range(16):
+            f_cut[q, j] = f_wide[q, pl.ds(j, 32, stride=16), :].astype(BF16).reshape(2, 16, 128)
     own = pltpu.make_async_copy(f_cut.at[y], buf.at[:, :, 0, z], own_sem)
     own.start()
 
-    @pl.when(row >= second_root)
-    def _():
-        pl.semaphore_wait(barrier, 2 + NY - 1 + NROW - 1)
-
-    @pl.when(row < second_root)
-    def _():
-        pl.semaphore_wait(barrier, 2 + NY - 1 + 2)
+    def span(c):
+        return pl.ds(BOUNDS[c], BOUNDS[c + 1] - BOUNDS[c])
 
     def y_copy(c, d):
         to = (y + d) % NY
         return remote(
-            f_cut.at[to, c], buf.at[c, :, NY - d, z], ysend.at[c, d - 1], yrecv.at[c, d - 1], at(row, to, z)
+            f_cut.at[to, span(c)], buf.at[span(c), :, NY - d, z],
+            ysend.at[c, d - 1], yrecv.at[c, d - 1], at(row, to, z),
         )
 
     def own_copy(part, way):
-        chunks = pl.ds(0, 1) if part == 0 else pl.ds(1, CHUNKS - 1)
-        return remote(
-            f_cut.at[y, chunks], buf.at[chunks, :, 0, z], osend.at[part, way], orecv.at[part, way],
+        blocks = span(0) if part == 0 else pl.ds(BOUNDS[1], 16 - BOUNDS[1])
+        return remote(
+            f_cut.at[y, blocks], buf.at[blocks, :, 0, z], osend.at[part, way], orecv.at[part, way],
             at(row, y, up if way == 0 else down),
         )
 
-    for c in range(CHUNKS):
-        for d in range(1, NY):
-            y_copy(c, d).start()
-        if c < 2:
-            for way in range(2):
-                own_copy(c, way).start()
+    def piece_y_copy(d):
+        to = (y + d) % NY
+        return remote(
+            f_cut.at[to, 15, 0], edge_f.at[NY - d, z], pysend.at[d - 1], pyrecv.at[d - 1], at(row, to, z)
+        )
+
+    def piece_z_copy(d):
+        return remote(
+            edge_f.at[:, z], edge_f.at[:, z], pzsend.at[d - 1], pzrecv.at[d - 1], at(row, y, (z + d) % NZ)
+        )
 
     def block_of_rhs(j):
         return jnp.concatenate(
@@ -126,8 +132,7 @@
         dot = functools.partial(jnp.dot, preferred_element_type=F32)
         return dot(high, d_cut[0]) + (dot(high, d_cut[1]) + dot(rest, d_cut[0]))
 
-    def spread_row(s, value, root):
-        nar[s, y], low[s] = halves(value)
+    def spread_row(s, root):
         for part in range(2):
             for t in ROW_TARGETS:
                 if t != root:
@@ -175,18 +180,41 @@
 
     @pl.when(row == first_root)
     def _():
-        spread_row(0, times_inverse(block_of_rhs(15)), first_root)
+        nar[0, y], low[0] = halves(times_inverse(block_of_rhs(15)))
+
+    @pl.when(row == first_root)
+    def _():
+        pl.semaphore_wait(barrier, 2 + NY - 1 + NROW - 1)
+        spread_row(0, first_root)
+
+    @pl.when(row == second_root)
+    def _():
+        pl.semaphore_wait(barrier, 2 + NY - 1 + NROW - 1 + len(FAR))
+        for d in range(1, NY):
+            piece_y_copy(d).start()
+        edge_f[0, z] = f_cut[y, 15, 0]
+
+    @pl.when(row < second_root)
+    def _():
+        pl.semaphore_wait(barrier, 2 + NY - 1 + 2)
+
+    for c in range(CHUNKS):
+        for d in range(1, NY):
+            y_copy(c, d).start()
+        if c < 2:
+            for way in range(2):
+                own_copy(c, way).start()
 
     def hop_copy(unit, hop, way):
         c, s = unit
         n = c * 2 + s
         block = (z - (hop - 1) + NZ) % NZ if way == 0 else (z + hop - 1) % NZ
         if hop == 1:
-            ref = buf.at[c, s, pl.ds(1, NY - 1), block]
+            ref = buf.at[span(c), s, pl.ds(1, NY - 1), block]
         elif hop < 4:
-            ref = buf.at[c, s, :, block]
+            ref = buf.at[span(c), s, :, block]
         else:
-            ref = buf.at[c, s, pl.ds(2 * way, 2), block]
+            ref = buf.at[span(c), s, pl.ds(2 * way, 2), block]
         return remote(
             ref, ref, zsend.at[way, n, hop - 1], zrecv.at[way, n, hop - 1],
             at(row, y, up if way == 0 else down),
@@ -194,26 +222,24 @@
 
     def edge_copy(d):
         to = (y + d) % NY
-        return remote(edge_out.at[to], edge_in, esend.at[d - 1], erecv.at[0], at(row, to, z))
+        return remote(edge_out.at[to], edge_in.at[y], esend.at[d - 1], erecv.at[d - 1], at(row, to, z))
 
     def back_copy(c, d):
         to = (y + d) % NY
         return remote(
-            back_out.at[c, to], back_in.at[c, y], bsend.at[c, d - 1], brecv.at[c, d - 1], at(row, to, z)
-        )
-
-    is_edge = jnp.logical_and(row == second_root, y == NY - 1)
+            back_out.at[to, span(c)], back_in.at[y, span(c)], bsend.at[c, d - 1], brecv.at[c, d - 1], at(row, to, z)
+        )
 
     def wait_last(unit):
         for way in range(2):
             hop_copy(unit, 4, way).wait_recv()
 
-    def subtract(j, change):
-        for l in range(4):
-            rows = pl.ds(4 * j + l, 64, stride=64)
-            upd_ref[rows, :] = x_v[rows, :] - change[:, l * 128:(l + 1) * 128].astype(F32)
+    def subtract(j, q, change):
+        rows = pl.ds(4 * j + q, 64, stride=64)
+        upd_ref[rows, :] = x_v[rows, :] - change.astype(F32)
 
     own_seen, y_seen = set(), set()
+    multiplied = stored = False
     own.wait()
     for step in ORDER:
         if step[0] in UNITS and len(step) == 2:
@@ -228,74 +254,103 @@
                 own_seen.add(min(c, 1))
                 for way in range(2):
                     own_copy(min(c, 1), way).wait_recv()
-            if step == "A3":
-                share_narrow(0, first_root)
             for way in range(2):
                 if hop > 1:
                     hop_copy(unit, hop - 1, way).wait_recv()
                 hop_copy(unit, hop, way).start()
+        elif step == "e0":
+
+            @pl.when(row >= second_root)
+            def _():
+                share_narrow(0, first_root)
+
+        elif step == "e1":
+
+            @pl.when(row == second_root)
+            def _():
+                for d in range(1, NY):
+                    piece_y_copy(d).wait_recv()
+                for d in range(1, NZ):
+                    piece_z_copy(d).start()
+
+        elif step == "n0":
+
+            @pl.when(row < second_root)
+            def _():
+                share_narrow(0, first_root)
+
         elif step == "edge":
-            take_narrow(0)
-            wait_last((0, 0))
-
-            @pl.when(is_edge)
+
+            @pl.when(row == second_root)
             def _():
+                take_narrow(0)
+                for d in range(1, NZ):
+                    piece_z_copy(d).wait_recv()
                 product = jnp.dot(
-                    lhs[:, :512], buf[0, 0].reshape(512, 512), preferred_element_type=F32
+                    lhs[:, :512], edge_f[...].reshape(512, 128), preferred_element_type=F32
                 )
-                edge_out[...] = product.reshape(NY, 64, 512)
+                edge_out[...] = product.reshape(NY, 64, 128)
                 for d in range(1, NY):
                     edge_copy(d).start()
-                edge_in[...] = edge_out[NY - 1]
-
-            store_solved(0, first_root)
+                edge_in[y] = edge_out[y]
 
         elif step == "solve":
 
             @pl.when(row == second_root)
             def _():
-                @pl.when(y != NY - 1)
-                def _():
-                    edge_copy(1).wait_recv()
-
-                spread_row(1, times_inverse(block_of_rhs(15) - edge_in[...]), second_root)
+                for d in range(1, NY):
+                    edge_copy(d).wait_recv()
+                change = jnp.concatenate([edge_in[q] for q in range(NY)], axis=1)
+                nar[1, y], low[1] = halves(times_inverse(block_of_rhs(15) - change))
+                spread_row(1, second_root)
 
         elif step == "share":
             share_narrow(1, second_root)
         elif step[0] == "c":
             c = int(step[1])
-            if c == 0:
+            if not multiplied:
+                multiplied = True
+
+                @pl.when(row != second_root)
+                def _():
+                    take_narrow(0)
+
                 take_narrow(1)
             for s in range(2):
-                if (c, s) != (0, 0):
-                    wait_last((c, s))
-            change = jnp.dot(lhs[...], buf[c].reshape(1024, 512), preferred_element_type=F32)
-            back_out[c] = change.astype(BF16).reshape(NY, 64, 512)
+                wait_last((c, s))
+            for j in range(BOUNDS[c], BOUNDS[c + 1], 2):
+                width = min(2, BOUNDS[c + 1] - j)
+                factor = jnp.concatenate([buf[j + i].reshape(1024, 128) for i in range(width)], axis=1)
+                change = jnp.dot(lhs[...], factor, preferred_element_type=F32).astype(BF16)
+                for i in range(width):
+                    back_out[:, j + i] = change[:, i * 128:(i + 1) * 128].reshape(NY, 64, 128)
             for d in range(1, NY):
                 back_copy(c, d).start()
-            back_in[c, y] = back_out[c, y]
         else:
             c = int(step[1])
-            if c == 0:
-                store_solved(1, second_root)
+            if not stored:
+                stored = True
+                for s in range(2):
+                    store_solved(s, NROW - 1 - s)
             for d in range(1, NY):
                 back_copy(c, d).wait_recv()
+            back_in[y, span(c)] = back_out[y, span(c)]
             for q in range(NY):
-                j = 4 * q + 3 - c
-                if j < 15:
-                    subtract(j, back_in[c, q])
-                else:
-                    @pl.when(row < second_root)
-                    def _():
-                        subtract(15, back_in[0, NY - 1])
-
-                    @pl.when(row == second_root)
-                    def _():
-                        subtract(15, edge_in[...])
-
-                    @pl.when(row == first_root)
-                    def _():
-                        subtract(15, jnp.zeros((64, 512), F32))
+                for j in range(BOUNDS[c], BOUNDS[c + 1]):
+                    if j < 15:
+                        subtract(j, q, back_in[q, j])
+                    else:
+                        @pl.when(row < second_root)
+                        def _(q=q):
+                            subtract(15, q, back_in[q, 15])
+
+                        @pl.when(row == second_root)
+                        def _(q=q):
+                            subtract(15, q, edge_in[q])
+
+                        @pl.when(row == first_root)
+                        def _(q=q):
+                            subtract(15, q, jnp.zeros((64, 128), F32))
 
     for c in range(CHUNKS):
         for d in range(1, NY):
@@ -321,10 +376,13 @@
                     if t != root:
                         row_copy(s, part, t).wait_send()
 
-    @pl.when(is_edge)
-    def _():
-        for d in range(1, NY):
+    @pl.when(row == second_root)
+    def _():
+        for d in range(1, NY):
+            piece_y_copy(d).wait_send()
             edge_copy(d).wait_send()
+        for d in range(1, NZ):
+            piece_z_copy(d).wait_send()
 
 
 def on_device(rhs, factor_rows, diag_inverse):
@@ -343,17 +401,18 @@
             pltpu.VMEM((4096, 128), F32),
             pltpu.VMEM((512, 512), BF16),
             pltpu.VMEM((4, 512, 128), F32),
-            pltpu.VMEM((NY, CHUNKS, 2, 16, 512), BF16),
+            pltpu.VMEM((NY, 16, 2, 16, 128), BF16),
             pltpu.VMEM((512, 512), F32),
             pltpu.VMEM((2, 512, 512), BF16),
-            pltpu.VMEM((CHUNKS, 2, NY, NZ, 16, 512), BF16),
+            pltpu.VMEM((16, 2, NY, NZ, 16, 128), BF16),
+            pltpu.VMEM((NY, NZ, 16, 128), BF16),
             pltpu.VMEM((2, NY, 64, 512), BF16),
             pltpu.VMEM((256, 1024), BF16),
             pltpu.VMEM((2, 64, 512), BF16),
-            pltpu.VMEM((NY, 64, 512), F32),
-            pltpu.VMEM((64, 512), F32),
-            pltpu.VMEM((CHUNKS, NY, 64, 512), BF16),
-            pltpu.VMEM((CHUNKS, NY, 64, 512), BF16),
+            pltpu.VMEM((NY, 64, 128), F32),
+            pltpu.VMEM((NY, 64, 128), F32),
+            pltpu.VMEM((NY, 16, 64, 128), BF16),
+            pltpu.VMEM((NY, 16, 64, 128), BF16),
             dma((3,)),
             dma,
             dma((CHUNKS, NY - 1)),
@@ -367,7 +426,11 @@
             dma((2, NY - 1)),
             dma((2, NY - 1)),
             dma((NY - 1,)),
-            dma((1,)),
+            dma((NY - 1,)),
+            dma((NY - 1,)),
+            dma((NY - 1,)),
+            dma((NZ - 1,)),
+            dma((NZ - 1,)),
             dma((CHUNKS, NY - 1)),
             dma((CHUNKS, NY - 1)),
         ],

time: 67.3 us -> 68 us (1.010)
  the two profiles are of different devices: /device:TPU:4 before, /device:TPU:6 now
where the time goes in v3:
time: 68 us; the launch traced here: 67.9 us
  Pallas kernels  65.2 us (96%)
  local copies, waits for them, and re-layouts  2.02 us (3%)
    pallas_call x1, Pallas kernels, on_device(): pl.pallas_call(kernel, out_shape=(pltpu.VMEM((2, 64, 512), F32), pltpu.VM...  65.2 us
    unnamed x2, local copies, waits for them, and re-layouts  2.02 us

profile of v3, /device:TPU:6, one launch (start us, length us, event | category | flops | bytes accessed | tf_op | source)
XLA Modules:
  0.0 67.9 jit_solution(5116074694974845439)
XLA Ops:
  0.6 65.2 %back_substitution.1 = (f32[2,64,512]{2,1,0:T(8,128)S(1)}, f32[4096,128]{1,0:T(8,128)S(1)}) custom-call(f32[4096,128]{1,0:T(8,128)} %bitcast.4, bf16[512,512]{1,0:T(8,128)(2,1)} %bitcast.5, f32[2,512,512]{2,1,0:T(8,128)} %d_hbm.1), custom_call_target="tpu_custom_call" | custom-call | tf_op jit(solution)/shard_map/back_substitution/pallas_call | solution.py:392
  65.9 0.7 %copy.8 = f32[2,64,512]{2,1,0:T(8,128)} copy(f32[2,64,512]{2,1,0:T(8,128)S(1)} %get-tuple-element.8) | data formatting | bytes 524288
  66.6 1.3 %copy.9 = f32[64,16,1,512]{3,2,1,0:T(1,128)} copy(f32[64,16,1,512]{3,2,1,0:T(1,128)S(1)} %bitcast.3) | data formatting | bytes 4194304

commit v4 on v3

--- a/solution.py
+++ b/solution.py
@@ -15,10 +15,10 @@
 BF16, F32 = jnp.bfloat16, jnp.float32
 BOUNDS = (0, 5, 10, 14, 16)
 ORDER = (
-    "A1", "B1", "C1", "e0", "G1", "D1", "e1", "H1", "C2", "D2", "edge",
-    "G2", "B2", "E1", "A2", "D3", "F1", "B3", "C3", "solve", "D4", "A3",
-    "E2", "n0", "F2", "C4", "share", "A4", "B4", "F3", "E3", "H2", "c1",
-    "G3", "c0", "F4", "E4", "H3", "G4", "c2", "H4", "c3", "f0", "f1",
+    "e1", "A1", "B1", "e0", "D1", "A2", "G1", "H1", "E1", "B2", "C1",
+    "n0", "A3", "D2", "edge", "C2", "A4", "E2", "solve", "B3", "F1", "C3",
+    "D3", "share", "B4", "G2", "F2", "D4", "H2", "C4", "E3", "c0", "F3",
+    "H3", "G3", "c1", "E4", "F4", "H4", "G4", "c2", "c3", "f0", "f1",
     "f2", "f3",
 )
 

time: 68 us -> 64.3 us (0.946)
  Pallas kernels: 65.2 us -> 61.6 us
    pallas_call x1, Pallas kernels: 65.2 us -> 61.6 us  [on_device(): pl.pallas_call(kernel, out_shape=(pltpu.VMEM((2, 64, 512), F32), pltpu.VM...]
where the time goes in v4:
time: 64.3 us
  Pallas kernels  61.6 us (96%)
  local copies, waits for them, and re-layouts  2.02 us (3%)
    pallas_call x1, Pallas kernels, on_device(): pl.pallas_call(kernel, out_shape=(pltpu.VMEM((2, 64, 512), F32), pltpu.VM...  61.6 us
    unnamed x2, local copies, waits for them, and re-layouts  2.02 us

profile of v4, /device:TPU:6, one launch (start us, length us, event | category | flops | bytes accessed | tf_op | source)
XLA Modules:
  0.0 64.3 jit_solution(15956085116807956551)
XLA Ops:
  0.6 61.6 %back_substitution.1 = (f32[2,64,512]{2,1,0:T(8,128)S(1)}, f32[4096,128]{1,0:T(8,128)S(1)}) custom-call(f32[4096,128]{1,0:T(8,128)} %bitcast.4, bf16[512,512]{1,0:T(8,128)(2,1)} %bitcast.5, f32[2,512,512]{2,1,0:T(8,128)} %d_hbm.1), custom_call_target="tpu_custom_call" | custom-call | tf_op jit(solution)/shard_map/back_substitution/pallas_call | solution.py:392
  62.2 0.7 %copy.8 = f32[2,64,512]{2,1,0:T(8,128)} copy(f32[2,64,512]{2,1,0:T(8,128)S(1)} %get-tuple-element.8) | data formatting | bytes 524288
  62.9 1.3 %copy.9 = f32[64,16,1,512]{3,2,1,0:T(1,128)} copy(f32[64,16,1,512]{3,2,1,0:T(1,128)S(1)} %bitcast.3) | data formatting | bytes 4194304

commit v5 on v4

--- a/solution.py
+++ b/solution.py
@@ -13,9 +13,9 @@
 ROW_TARGETS = (6, 2, 3, 0, 1, 4, 5, 7)
 FAR = (2, 3, 4, 5, 6)
 BF16, F32 = jnp.bfloat16, jnp.float32
-BOUNDS = (0, 5, 10, 14, 16)
+BOUNDS = (0, 5, 9, 13, 16)
 ORDER = (
-    "e1", "A1", "B1", "e0", "D1", "A2", "G1", "H1", "E1", "B2", "C1",
+    "e1", "A1", "B1", "e0", "E1", "D1", "A2", "G1", "H1", "B2", "C1",
     "n0", "A3", "D2", "edge", "C2", "A4", "E2", "solve", "B3", "F1", "C3",
     "D3", "share", "B4", "G2", "F2", "D4", "H2", "C4", "E3", "c0", "F3",
     "H3", "G3", "c1", "E4", "F4", "H4", "G4", "c2", "c3", "f0", "f1",
@@ -45,6 +45,13 @@
             device_id=device, device_id_type=pl.DeviceIdType.MESH,
         )
 
+    f_in = pltpu.make_async_copy(f_hbm, f_v, in_sem.at[0])
+    x_in = pltpu.make_async_copy(x_hbm, x_v, in_sem.at[1])
+    d_in = pltpu.make_async_copy(d_hbm.at[jnp.where(row == first_root, 0, 1)], d_v, in_sem.at[2])
+    f_in.start()
+    d_in.start()
+    x_in.start()
+
     def signal(device):
         pl.semaphore_signal(barrier, inc=1, device_id=device, device_id_type=pl.DeviceIdType.MESH)
 
@@ -74,13 +81,6 @@
         for d in FAR:
             signal(at(row, y, (z + d) % NZ))
 
-    f_in = pltpu.make_async_copy(f_hbm, f_v, in_sem.at[0])
-    x_in = pltpu.make_async_copy(x_hbm, x_v, in_sem.at[1])
-    d_in = pltpu.make_async_copy(d_hbm.at[jnp.where(row == first_root, 0, 1)], d_v, in_sem.at[2])
-    f_in.start()
-    d_in.start()
-    x_in.start()
-
     f_in.wait()
     for l in range(4):
         f_wide[l] = f_v[:, l * 128:(l + 1) * 128].astype(F32)
@@ -169,23 +169,9 @@
 
         sol_ref[s] = nar[s, y].astype(F32) + low[s].astype(F32)
 
-    d_in.wait()
-    x_in.wait()
-
-    @pl.when(row >= second_root)
-    def _():
-        for i in range(4):
-            rows = slice(i * 128, (i + 1) * 128)
-            d_cut[0, rows], d_cut[1, rows] = halves(d_v[rows])
-
     @pl.when(row == first_root)
     def _():
-        nar[0, y], low[0] = halves(times_inverse(block_of_rhs(15)))
-
-    @pl.when(row == first_root)
-    def _():
         pl.semaphore_wait(barrier, 2 + NY - 1 + NROW - 1)
-        spread_row(0, first_root)
 
     @pl.when(row == second_root)
     def _():
@@ -204,6 +190,20 @@
         if c < 2:
             for way in range(2):
                 own_copy(c, way).start()
+
+    d_in.wait()
+    x_in.wait()
+
+    @pl.when(row >= second_root)
+    def _():
+        for i in range(4):
+            rows = slice(i * 128, (i + 1) * 128)
+            d_cut[0, rows], d_cut[1, rows] = halves(d_v[rows])
+
+    @pl.when(row == first_root)
+    def _():
+        nar[0, y], low[0] = halves(times_inverse(block_of_rhs(15)))
+        spread_row(0, first_root)
 
     def hop_copy(unit, hop, way):
         c, s = unit

time: 64.3 us -> 64 us (level)
  the two profiles are of different devices: /device:TPU:6 before, /device:TPU:4 now
where the time goes in v5:
time: 64 us
  Pallas kernels  61.3 us (96%)
  local copies, waits for them, and re-layouts  2.02 us (3%)
  between operations  0.64 us (1%)
    pallas_call x1, Pallas kernels, on_device(): pl.pallas_call(kernel, out_shape=(pltpu.VMEM((2, 64, 512), F32), pltpu.VM...  61.3 us
    unnamed x2, local copies, waits for them, and re-layouts  2.02 us

profile of v5, /device:TPU:4, one launch (start us, length us, event | category | flops | bytes accessed | tf_op | source)
XLA Modules:
  0.0 64.0 jit_solution(1774662342792349113)
XLA Ops:
  0.6 61.3 %back_substitution.1 = (f32[2,64,512]{2,1,0:T(8,128)S(1)}, f32[4096,128]{1,0:T(8,128)S(1)}) custom-call(f32[4096,128]{1,0:T(8,128)} %bitcast.4, bf16[512,512]{1,0:T(8,128)(2,1)} %bitcast.5, f32[2,512,512]{2,1,0:T(8,128)} %d_hbm.1), custom_call_target="tpu_custom_call" | custom-call | tf_op jit(solution)/shard_map/back_substitution/pallas_call | solution.py:392
  61.9 0.7 %copy.8 = f32[2,64,512]{2,1,0:T(8,128)} copy(f32[2,64,512]{2,1,0:T(8,128)S(1)} %get-tuple-element.8) | data formatting | bytes 524288
  62.6 1.3 %copy.9 = f32[64,16,1,512]{3,2,1,0:T(1,128)} copy(f32[64,16,1,512]{3,2,1,0:T(1,128)S(1)} %bitcast.3) | data formatting | bytes 4194304

commit v6 on v5

--- a/solution.py
+++ b/solution.py
@@ -12,6 +12,7 @@
 UNITS = "ABCDEFGH"
 ROW_TARGETS = (6, 2, 3, 0, 1, 4, 5, 7)
 FAR = (2, 3, 4, 5, 6)
+FARTHEST_FIRST = (2, 1, 3)
 BF16, F32 = jnp.bfloat16, jnp.float32
 BOUNDS = (0, 5, 9, 13, 16)
 ORDER = (
@@ -324,7 +325,7 @@
                 change = jnp.dot(lhs[...], factor, preferred_element_type=F32).astype(BF16)
                 for i in range(width):
                     back_out[:, j + i] = change[:, i * 128:(i + 1) * 128].reshape(NY, 64, 128)
-            for d in range(1, NY):
+            for d in FARTHEST_FIRST:
                 back_copy(c, d).start()
         else:
             c = int(step[1])

time: 64 us -> 63.8 us (level)
  no operation moved by 1% of the time
where the time goes in v6:
time: 63.8 us; the launch traced here: 63.7 us
  Pallas kernels  61.1 us (96%)
  local copies, waits for them, and re-layouts  2.02 us (3%)
  between operations  0.64 us (1%)
    pallas_call x1, Pallas kernels, on_device(): pl.pallas_call(kernel, out_shape=(pltpu.VMEM((2, 64, 512), F32), pltpu.VM...  61.1 us
    unnamed x2, local copies, waits for them, and re-layouts  2.02 us

profile of v6, /device:TPU:4, one launch (start us, length us, event | category | flops | bytes accessed | tf_op | source)
XLA Modules:
  0.0 63.7 jit_solution(9180754309780191930)
XLA Ops:
  0.6 61.1 %back_substitution.1 = (f32[2,64,512]{2,1,0:T(8,128)S(1)}, f32[4096,128]{1,0:T(8,128)S(1)}) custom-call(f32[4096,128]{1,0:T(8,128)} %bitcast.4, bf16[512,512]{1,0:T(8,128)(2,1)} %bitcast.5, f32[2,512,512]{2,1,0:T(8,128)} %d_hbm.1), custom_call_target="tpu_custom_call" | custom-call | tf_op jit(solution)/shard_map/back_substitution/pallas_call | solution.py:393
  61.7 0.7 %copy.8 = f32[2,64,512]{2,1,0:T(8,128)} copy(f32[2,64,512]{2,1,0:T(8,128)S(1)} %get-tuple-element.8) | data formatting | bytes 524288
  62.4 1.3 %copy.9 = f32[64,16,1,512]{3,2,1,0:T(1,128)} copy(f32[64,16,1,512]{3,2,1,0:T(1,128)S(1)} %bitcast.3) | data formatting | bytes 4194304

commit v7 on v6

--- a/solution.py
+++ b/solution.py
@@ -152,7 +152,7 @@
         def _():
             row_copy(s, 0, 0).wait_recv()
 
-        for d in range(1, NY):
+        for d in FARTHEST_FIRST:
             narrow_copy(s, d).start()
 
     def take_narrow(s):
@@ -186,7 +186,7 @@
         pl.semaphore_wait(barrier, 2 + NY - 1 + 2)
 
     for c in range(CHUNKS):
-        for d in range(1, NY):
+        for d in FARTHEST_FIRST:
             y_copy(c, d).start()
         if c < 2:
             for way in range(2):

time: 63.8 us -> 63.8 us (level)
  no operation moved by 1% of the time
where the time goes in v7:
time: 63.8 us; the launch traced here: 63.7 us
  Pallas kernels  61.1 us (96%)
  local copies, waits for them, and re-layouts  2.02 us (3%)
  between operations  0.64 us (1%)
    pallas_call x1, Pallas kernels, on_device(): pl.pallas_call(kernel, out_shape=(pltpu.VMEM((2, 64, 512), F32), pltpu.VM...  61.1 us
    unnamed x2, local copies, waits for them, and re-layouts  2.02 us

profile of v7, /device:TPU:4, one launch (start us, length us, event | category | flops | bytes accessed | tf_op | source)
XLA Modules:
  0.0 63.7 jit_solution(2217628471892536549)
XLA Ops:
  0.6 61.1 %back_substitution.1 = (f32[2,64,512]{2,1,0:T(8,128)S(1)}, f32[4096,128]{1,0:T(8,128)S(1)}) custom-call(f32[4096,128]{1,0:T(8,128)} %bitcast.4, bf16[512,512]{1,0:T(8,128)(2,1)} %bitcast.5, f32[2,512,512]{2,1,0:T(8,128)} %d_hbm.1), custom_call_target="tpu_custom_call" | custom-call | tf_op jit(solution)/shard_map/back_substitution/pallas_call | solution.py:393
  61.7 0.7 %copy.8 = f32[2,64,512]{2,1,0:T(8,128)} copy(f32[2,64,512]{2,1,0:T(8,128)S(1)} %get-tuple-element.8) | data formatting | bytes 524288
  62.4 1.3 %copy.9 = f32[64,16,1,512]{3,2,1,0:T(1,128)} copy(f32[64,16,1,512]{3,2,1,0:T(1,128)S(1)} %bitcast.3) | data formatting | bytes 4194304
